TPU v7x, 128 devices: a whole 4x4x4 slice. The times are simulated.
128 devices in a mesh: narrow: 4 (over y_hi, core), wide: 32 (over z, y_lo, x).
Axes of the slice: x: 4, y: 4 (y_hi: 2, y_lo: 2; y = y_hi * 2 + y_lo), z: 4, core: 2. Of those that a mesh axis runs over, the one named last changes fastest.
Arguments:
- velocity: float32 [3, 384, 512, 512], P(None, None, 'wide', 'narrow'), may hold values from -6 to 6
- inv_spacing: float32 [384], replicated, may hold values from 0.5 to 2
- eigen_wall: float32 [384], P(('narrow', 'wide')), may hold values from 0.01 to 1
- to_modes: float32 [384, 384], replicated, may hold values from -1 to 2
- from_modes: float32 [384, 384], replicated, may hold values from -1 to 2
Outputs:
- new_velocity: float32 [3, 384, 512, 512], P(None, None, 'wide', 'narrow')
All inputs are finite; a program needn't handle non-finite values.
Results may differ from a plain program's by a relative error of at most 0.035.
Values sent between devices are 32-bit elements; how exact they have to be, the bound alone decides.
A program may use at most 192 MiB of HBM per device.

v0:
```python
import functools
import math

import jax
import jax.numpy as jnp
import ml_dtypes
import numpy as np
from jax import lax
from jax.experimental import pallas as pl
from jax.experimental.pallas import tpu as pltpu
from jax.sharding import PartitionSpec as P

MESH = pl.DeviceIdType.MESH
LZ = 16
LX = 128
NY = 384
ROWS = NY * LZ
GROUPS = NY // LX


def first_kernel(nn, nb, v_hbm, spacing, eig, star_hbm, source, walls,
                 v, star, src, zsend, zrecv, xsend, xrecv, s2send, s2recv, x0send, x0recv,
                 load_sem, store_sem, z_ss, z_rs, x_ss, x_rs, s2_ss, s2_rs, x0_ss, x0_rs, e_ss, e_rs):
    me_n = lax.axis_index("narrow")
    me_b = lax.axis_index("wide")
    ring = nb // 4
    layer = me_b // ring
    spot = lax.rem(me_b, ring)
    up = (me_n, lax.rem(me_b + 1, nb))
    down = (me_n, lax.rem(me_b + nb - 1, nb))
    right = (lax.rem(me_n + 1, nn), me_b)
    left = (lax.rem(me_n + nn - 1, nn), me_b)

    loads = [pltpu.make_async_copy(v_hbm.at[c], v.at[c, pl.ds(LZ, ROWS)], load_sem.at[c]) for c in range(3)]
    for c in (2, 0, 1):
        loads[c].start()

    barrier = pltpu.get_barrier_semaphore()
    narrow_peers = [(lax.rem(me_n + k, nn), me_b) for k in range(1, nn)]
    spot_peers = [(me_n, layer * ring + lax.rem(spot + k, ring)) for k in range(1, ring)]
    layer_peers = [(me_n, lax.rem(layer + k, 4) * ring + spot) for k in range(1, 4)]
    greeted = [up, down] + narrow_peers + spot_peers + layer_peers
    for peer in greeted:
        pl.semaphore_signal(barrier, inc=1, device_id=peer, device_id_type=MESH)

    zero = jnp.zeros((LZ, LX), jnp.float32)
    for c in range(3):
        v[c, pl.ds(0, LZ), :] = zero
        v[c, pl.ds(LZ + ROWS, LZ), :] = zero
        star[c, pl.ds(0, LZ), :] = zero
        star[c, pl.ds(LZ + ROWS, LZ), :] = zero
    lane1 = lax.broadcasted_iota(jnp.int32, (1, LX), 1)
    row = jnp.where(lane1 == 0, eig[0], jnp.where(lane1 == 1, eig[1], jnp.where(lane1 == 2, eig[2], 0.0)))
    my_wall = me_b * nn + me_n
    walls[my_wall] = row
    pl.semaphore_wait(barrier, len(greeted))

    def share(peers, at, count, stage):
        for k, peer in enumerate(peers):
            pltpu.make_async_remote_copy(
                src_ref=walls.at[pl.ds(at, count)], dst_ref=walls.at[pl.ds(at, count)],
                send_sem=e_ss.at[stage], recv_sem=e_rs.at[stage], device_id=peer, device_id_type=MESH).start()

    def share_wait(peers, count, stage):
        n = len(peers) * count
        w = pltpu.make_async_remote_copy(
            src_ref=walls.at[pl.ds(0, n)], dst_ref=walls.at[pl.ds(0, n)],
            send_sem=e_ss.at[stage], recv_sem=e_rs.at[stage], device_id=peers[0], device_id_type=MESH)
        w.wait_send()
        w.wait_recv()

    def remote(src_ref, dst_ref, ss, rs, peer):
        return pltpu.make_async_remote_copy(src_ref=src_ref, dst_ref=dst_ref, send_sem=ss, recv_sem=rs,
                                            device_id=peer, device_id_type=MESH)

    lane = lax.broadcasted_iota(jnp.int32, (LZ, LX), 1)
    level = lax.broadcasted_iota(jnp.int32, (LZ, LX), 0)

    def pack(ref, c, g):
        def step(yy, carry):
            last, first = carry
            plane = ref[c, pl.ds(pl.multiple_of(LZ + (g * LX + yy) * LZ, LZ), LZ), :]
            turned = pltpu.roll(plane, lax.rem(yy + 1, LX), 1)
            last = jnp.where(lane == yy, turned, last)
            first = jnp.where(lane == lax.rem(yy + 1, LX), turned, first)
            return last, first
        last, first = lax.fori_loop(0, LX, step, (zero, zero), unroll=8)
        return last, pltpu.roll(first, LX - 1, 1)

    share(narrow_peers, my_wall, 1, 0)
    zcopies, xcopies = [], []
    for c in (2, 0, 1):
        loads[c].wait()
        zsend[0, c] = v[c, pl.ds(LZ + LZ - 1, NY, stride=LZ), :]
        zsend[1, c] = v[c, pl.ds(LZ, NY, stride=LZ), :]
        for side, peer in ((0, up), (1, down)):
            cp = remote(zsend.at[side, c], zrecv.at[side, c], z_ss.at[side, c], z_rs.at[side, c], peer)
            cp.start()
            zcopies.append(cp)
        for g in range(GROUPS):
            last, first = pack(v, c, g)
            xsend[0, c, g] = last
            xsend[1, c, g] = first
        for side, peer in ((0, right), (1, left)):
            cp = remote(xsend.at[side, c], xrecv.at[side, c], x_ss.at[side, c], x_rs.at[side, c], peer)
            cp.start()
            xcopies.append(cp)

    share_wait(narrow_peers, 1, 0)
    share(spot_peers, me_b * nn, nn, 1)
    for cp in xcopies:
        cp.wait_recv()

    def predict_plane(y, _):
        g = y // LX
        yy = lax.rem(y, LX)
        base = pl.multiple_of(LZ + y * LZ, LZ)
        s = spacing[y]
        centre = [v[c, pl.ds(base, LZ), :] for c in range(3)]
        a_e = 0.05 - 0.05 * centre[0]
        a_w = 0.05 + 0.05 * centre[0]
        a_n = jnp.where(level == LZ - 1, 0.0, 0.05 - 0.05 * centre[2])
        a_s = jnp.where(level == 0, 0.0, 0.05 + 0.05 * centre[2])
        curve = 0.05 * s * s
        slope = (0.05 * s) * centre[1]
        a_u = curve - slope
        a_l = curve + slope
        a_c = 0.8 - 2.0 * curve
        to_last = lax.rem(2 * LX - 1 - yy, LX)
        to_first = lax.rem(LX - yy, LX)
        for c in range(3):
            f = centre[c]
            upper = v[c, pl.ds(base + LZ, LZ), :]
            lower = v[c, pl.ds(base - LZ, LZ), :]
            north = pltpu.roll(f, LZ - 1, 0)
            south = pltpu.roll(f, 1, 0)
            east = jnp.where(lane == LX - 1, pltpu.roll(xrecv[1, c, g], to_last, 1), pltpu.roll(f, LX - 1, 1))
            west = jnp.where(lane == 0, pltpu.roll(xrecv[0, c, g], to_first, 1), pltpu.roll(f, 1, 1))
            star[c, pl.ds(base, LZ), :] = (
                a_c * f + a_e * east + a_w * west + (a_n * north + a_s * south) + (a_u * upper + a_l * lower))
        return 0

    lax.fori_loop(0, NY, predict_plane, 0, unroll=2)

    share_wait(spot_peers, nn, 1)
    share(layer_peers, layer * ring * nn, ring * nn, 2)
    for cp in zcopies:
        cp.wait_recv()
    part = 96
    for c in (2, 0, 1):
        for k in range(NY // part):
            hi = LZ + k * part * LZ + LZ - 1
            lo = LZ + k * part * LZ
            rows = pl.ds(k * part, part)
            top = star[c, pl.ds(hi, part, stride=LZ), :] + zrecv[1, c, rows, :] * (
                0.05 - 0.05 * v[2, pl.ds(hi, part, stride=LZ), :])
            low = star[c, pl.ds(lo, part, stride=LZ), :] + zrecv[0, c, rows, :] * (
                0.05 + 0.05 * v[2, pl.ds(lo, part, stride=LZ), :])
            star[c, pl.ds(hi, part, stride=LZ), :] = top
            star[c, pl.ds(lo, part, stride=LZ), :] = low
            if c == 2:
                s2send[0, rows, :] = top
                s2send[1, rows, :] = low
        if c == 2:
            s2copies = [remote(s2send.at[side], s2recv.at[side], s2_ss.at[side], s2_rs.at[side], peer)
                        for side, peer in ((0, up), (1, down))]
            for cp in s2copies:
                cp.start()
        if c == 0:
            for g in range(GROUPS):
                last, first = pack(star, 0, g)
                x0send[0, g] = last
                x0send[1, g] = first
            x0copies = [remote(x0send.at[side], x0recv.at[side], x0_ss.at[side], x0_rs.at[side], peer)
                        for side, peer in ((0, right), (1, left))]
            for cp in x0copies:
                cp.start()
    stores = [pltpu.make_async_copy(star.at[c, pl.ds(LZ, ROWS)], star_hbm.at[c], store_sem.at[c]) for c in range(3)]
    for cp in stores:
        cp.start()
    for cp in x0copies:
        cp.wait_recv()

    def diverge_plane(y, _):
        g = y // LX
        yy = lax.rem(y, LX)
        base = pl.multiple_of(LZ + y * LZ, LZ)
        s = 5.0 * spacing[y]
        to_last = lax.rem(2 * LX - 1 - yy, LX)
        to_first = lax.rem(LX - yy, LX)
        f = star[0, pl.ds(base, LZ), :]
        east = jnp.where(lane == LX - 1, pltpu.roll(x0recv[1, g], to_last, 1), pltpu.roll(f, LX - 1, 1))
        west = jnp.where(lane == 0, pltpu.roll(x0recv[0, g], to_first, 1), pltpu.roll(f, 1, 1))
        h = star[2, pl.ds(base, LZ), :]
        north = jnp.where(level == LZ - 1, 0.0, pltpu.roll(h, LZ - 1, 0))
        south = jnp.where(level == 0, 0.0, pltpu.roll(h, 1, 0))
        rise = star[1, pl.ds(base + LZ, LZ), :] - star[1, pl.ds(base - LZ, LZ), :]
        src[pl.ds(pl.multiple_of(y * LZ, LZ), LZ), :] = 5.0 * ((east - west) + (north - south)) + s * rise
        return 0

    lax.fori_loop(0, NY, diverge_plane, 0, unroll=4)
    for z in range(1, LZ - 1):
        source[z] = src[pl.ds(z, NY, stride=LZ), :]
    for cp in s2copies:
        cp.wait_recv()
    source[0] = src[pl.ds(0, NY, stride=LZ), :] - 5.0 * s2recv[0]
    source[LZ - 1] = src[pl.ds(LZ - 1, NY, stride=LZ), :] + 5.0 * s2recv[1]
    share_wait(layer_peers, ring * nn, 2)
    for cp in zcopies + xcopies + s2copies + x0copies:
        cp.wait_send()
    for cp in stores:
        cp.wait()


def first_part(velocity, inv_spacing, eigen_wall):
    nn, nb = lax.axis_size("narrow"), lax.axis_size("wide")
    f32 = jnp.float32
    any_, vmem, smem = (pl.BlockSpec(memory_space=m) for m in (pl.ANY, pltpu.VMEM, pltpu.SMEM))
    dma = pltpu.SemaphoreType.DMA
    return pl.pallas_call(
        functools.partial(first_kernel, nn, nb),
        out_shape=(jax.ShapeDtypeStruct((3, ROWS, LX), f32), jax.ShapeDtypeStruct((LZ, NY, LX), f32),
                   jax.ShapeDtypeStruct((nn * nb, 1, LX), f32)),
        in_specs=[any_, smem, smem],
        out_specs=(any_, vmem, vmem),
        scratch_shapes=[
            pltpu.VMEM((3, ROWS + 2 * LZ, LX), f32), pltpu.VMEM((3, ROWS + 2 * LZ, LX), f32), pltpu.VMEM((ROWS, LX), f32),
            pltpu.VMEM((2, 3, NY, LX), f32), pltpu.VMEM((2, 3, NY, LX), f32),
            pltpu.VMEM((2, 3, GROUPS, LZ, LX), f32), pltpu.VMEM((2, 3, GROUPS, LZ, LX), f32),
            pltpu.VMEM((2, NY, LX), f32), pltpu.VMEM((2, NY, LX), f32),
            pltpu.VMEM((2, GROUPS, LZ, LX), f32), pltpu.VMEM((2, GROUPS, LZ, LX), f32),
            dma((3,)), dma((3,)), dma((2, 3)), dma((2, 3)), dma((2, 3)), dma((2, 3)),
            dma((2,)), dma((2,)), dma((2,)), dma((2,)), dma((3,)), dma((3,)),
        ],
        compiler_params=pltpu.CompilerParams(collective_id=0, has_side_effects=True, vmem_limit_bytes=56 * 1024 * 1024),
        name="predict_diverge",
    )(velocity.reshape(3, ROWS, LX), inv_spacing, eigen_wall)


def split(a):
    high = a.astype(jnp.bfloat16)
    return high, (a - high.astype(jnp.float32)).astype(jnp.bfloat16)


def mm(a, b):
    return jnp.dot(a, b, preferred_element_type=jnp.float32)


def mm3(a, b_high, b_low):
    high, low = split(a)
    return mm(high, b_high) + mm(low, b_high) + mm(high, b_low)


def cosines(n):
    j = np.arange(n)[:, None]
    z = np.arange(n)[None, :]
    q = np.cos(np.pi * j * (z + 0.5) / n) * np.where(j == 0, math.sqrt(1 / n), math.sqrt(2 / n))
    return q, 2 - 2 * np.cos(np.pi * np.arange(n) / n)


def fourier(n):
    r = np.arange(n)[:, None]
    c = np.arange(n)[None, :]
    mid = n // 2
    k = np.where(r <= mid, r, r - mid)
    phase = (k * c % n) * (2 * np.pi / n)
    waves = np.where(r <= mid, np.cos(phase), np.sin(phase))
    weight = np.where((r == 0) | (r == mid), math.sqrt(1 / n), math.sqrt(2 / n))
    return waves * weight, 2 - 2 * np.cos(2 * np.pi * k[:, 0] / n)


def halves(a):
    a = np.asarray(a, np.float32)
    high = a.astype(ml_dtypes.bfloat16)
    return high, (a - high.astype(np.float32)).astype(ml_dtypes.bfloat16)


def paired(a):
    high, low = halves(a)
    return np.block([[high, low], [high, np.zeros_like(low)]])


QZ, NU = cosines(LZ)
QX, MU = cosines(LX)
QZL, QZF = QZ[:, -1], QZ[:, 0]
QXL, QXF = QX[:, -1], QX[:, 0]
SLOT = 2 * LZ
R = 3


def to_cosines(x):
    n = len(x)
    out = [None] * n
    e = [x[z] + x[n - 1 - z] for z in range(n // 2)]
    o = [x[z] - x[n - 1 - z] for z in range(n // 2)]
    ee = [e[z] + e[n // 2 - 1 - z] for z in range(n // 4)]
    eo = [e[z] - e[n // 2 - 1 - z] for z in range(n // 4)]
    for j in range(n):
        part = o if j % 2 else (eo if j % 4 else ee)
        out[j] = sum(float(QZ[j, z]) * part[z] for z in range(len(part)))
    return out


def from_cosines(f):
    n = len(f)
    even, out = [None] * (n // 2), [None] * n
    for z in range(n // 4):
        a = sum(float(QZ[j, z]) * f[j] for j in range(0, n, 4))
        b = sum(float(QZ[j, z]) * f[j] for j in range(2, n, 4))
        even[z], even[n // 2 - 1 - z] = a + b, a - b
    for z in range(n // 2):
        odd = sum(float(QZ[j, z]) * f[j] for j in range(1, n, 2))
        out[z], out[n - 1 - z] = even[z] + odd, even[z] - odd
    return out


def solve_kernel(nn, nb, source, to_modes, walls, own, mu_row, xw, edge_hl, edge_h, nu_lane, nu_row, mu_col, q_lane,
                 spec_h, spec_l, back_h, back_l, turn_h, turn_l, unturn_h, unturn_l, cos_b, ex_row,
                 fh, got, gz, gh, zl, zf, send, recv, back, s1, r1, s2, r2, loc):
    f32 = jnp.float32
    nd = nn * nb
    me_n = lax.axis_index("narrow")
    me_b = lax.axis_index("wide")
    me = me_n * nb + me_b
    barrier = pltpu.get_barrier_semaphore()

    def greet(k, _):
        d = lax.rem(me + k, nd)
        pl.semaphore_signal(barrier, inc=1, device_id=(d // nb, lax.rem(d, nb)), device_id_type=MESH)
        return 0

    lax.fori_loop(1, nd, greet, 0)

    t_high, t_low = split(to_modes[...])
    for z in range(0, LZ, 2):
        s_high, s_low = split(jnp.concatenate([source[z], source[z + 1]], axis=1))
        modal = mm(t_high, s_high) + mm(t_low, s_high) + mm(t_high, s_low)
        for k in range(2):
            high, low = split(modal[:, k * LX:(k + 1) * LX])
            both = mm(jnp.concatenate([high, low], axis=1), xw[...])
            gz[z + k] = both[:, :LX] + both[:, LX:]

    def chunk(k, _):
        rows = pl.ds(pl.multiple_of(k * 8, 8), 8)
        f = to_cosines([gz[z, rows, :] for z in range(LZ)])
        base = walls[rows, :] + mu_row[...]
        sums = [None, None]
        for j in range(LZ):
            fh[j, rows, :] = f[j]
            g = f[j] * pl.reciprocal(base + float(NU[j]))
            gh[j, rows, :] = g
            term = float(QZL[j]) * g
            sums[j % 2] = term if sums[j % 2] is None else sums[j % 2] + term
        zl[rows, :] = sums[0] + sums[1]
        zf[rows, :] = sums[0] - sums[1]
        return 0

    lax.fori_loop(0, NY // 8, chunk, 0)
    edge = jnp.zeros((NY, LX), f32)
    for j in range(0, LZ, 2):
        high, low = split(jnp.concatenate([gh[j], gh[j + 1]], axis=1))
        both = mm(high, edge_hl[j // 2])
        edge = edge + both[:, :LX] + both[:, LX:] + mm(low, edge_h[j // 2])
    packed = edge[:nd]
    for r in range(R):
        rows = pl.ds(r * nd, nd)
        send[pl.ds(r, nd, stride=8), :] = zl[rows, :]
        send[pl.ds(R + r, nd, stride=8), :] = zf[rows, :]
        if r:
            packed = packed + pltpu.roll(edge[r * nd:(r + 1) * nd], SLOT * r, 1)
    send[pl.ds(2 * R, nd, stride=8), :] = packed
    send[pl.ds(2 * R + 1, nd, stride=8), :] = jnp.zeros((nd, LX), f32)
    pl.semaphore_wait(barrier, nd - 1)

    def ship(src, dst, ss, rs):
        def go(k, _):
            d = lax.rem(me + k, nd)
            pltpu.make_async_remote_copy(
                src_ref=src.at[pl.ds(pl.multiple_of(d * 8, 8), 8)], dst_ref=dst.at[pl.ds(pl.multiple_of(me * 8, 8), 8)],
                send_sem=ss, recv_sem=rs, device_id=(d // nb, lax.rem(d, nb)), device_id_type=MESH).start()
            return 0
        lax.fori_loop(1, nd, go, 0)
        mine = pl.ds(pl.multiple_of(me * 8, 8), 8)
        dst[mine, :] = src[mine, :]
        most = pl.ds(0, (nd - 1) * 8)
        return pltpu.make_async_remote_copy(src_ref=src.at[most], dst_ref=dst.at[most], send_sem=ss, recv_sem=rs,
                                            device_id=(me_n, me_b), device_id_type=MESH)

    out = ship(send, recv, s1, r1)

    lane = lax.broadcasted_iota(jnp.int32, (1, LX), 1)
    owner_lane = jnp.where(lane < SLOT, own[0], jnp.where(lane < 2 * SLOT, own[1], own[2]))
    rowid = lax.broadcasted_iota(jnp.int32, (LX, LX), 0)
    owner_row = jnp.where(rowid < SLOT, own[0], jnp.where(rowid < 2 * SLOT, own[1], own[2]))
    low_half = lax.rem(lane, SLOT) < LZ
    d_rows = pl.reciprocal(owner_row + nu_row[...] + mu_row[...])
    d_cols = pl.reciprocal(owner_lane + nu_lane[...] + mu_col[...])
    qxl, qxf = q_lane[0:1], q_lane[1:2]
    qzl = jnp.where(low_half, q_lane[2:3], 0.0)
    qzf = jnp.where(low_half, q_lane[3:4], 0.0)
    hll = jnp.sum(d_cols * q_lane[8:8 + LX], axis=0, keepdims=True)
    hlf = jnp.sum(d_cols * q_lane[8 + LX:8 + 2 * LX], axis=0, keepdims=True)
    l0, l1, l2 = (1.0 / (1 + 2 * hll - 2 * hlf), 1.0 / (1 + 2 * hll), 1.0 / (1 + 2 * hll + 2 * hlf))
    k0, k1, k2 = (0.25 * (l0 + 2 * l1 + l2), 0.25 * (l0 - l2), 0.25 * (l0 - 2 * l1 + l2))
    dr_h, dr_l = split(d_rows)
    dc_h, dc_l = split(d_cols)
    scale = []
    for r in range(R):
        gll = jnp.zeros_like(ex_row[...])
        glf = jnp.zeros_like(ex_row[...])
        for j in range(LZ):
            g = 1.0 / (own[r] + float(NU[j]) + ex_row[...])
            gll = gll + float(QZL[j] ** 2) * g
            glf = glf + float(QZL[j] * QZF[j]) * g
        scale.append(1.0 / (1 + 2 * gll - 2 * glf * cos_b[...]))
    scale = jnp.concatenate(scale, axis=0)

    def coupled(a):
        return [k0 * a[n] + k1 * (a[(n + 1) % nn] + a[(n - 1) % nn]) + k2 * a[(n + 2) % nn] for n in range(nn)]

    def ahead(a):
        return pltpu.roll(a, nb - 1, 0)

    def behind(a):
        return pltpu.roll(a, 1, 0)

    def blocks(a):
        return [a[n * nb:(n + 1) * nb] for n in range(nn)]

    out.wait_recv()
    x = blocks(recv[pl.ds(2 * R, nd, stride=8), :])
    t = coupled([jnp.where(low_half, x[n] - pltpu.roll(x[(n + 1) % nn], LX - LZ, 1), 0.0) for n in range(nn)])
    big = jnp.concatenate([qzl * t[n] - qzf * ahead(t[n]) for n in range(nn)], axis=0)
    lines = []
    for r in range(R):
        mine = (lane >= SLOT * r) & (lane < SLOT * (r + 1))
        td = blocks(mm3(jnp.where(mine, big, 0.0), dr_h, dr_l))
        last = blocks(recv[pl.ds(r, nd, stride=8), :])
        first = blocks(recv[pl.ds(R + r, nd, stride=8), :])
        lines.append(jnp.concatenate(
            [last[n] - ahead(first[n]) - (qxl * td[n] - qxf * td[(n - 1) % nn]) for n in range(nn)], axis=1))
    s = mm3(jnp.concatenate(lines, axis=0), spec_h[...], spec_l[...])
    s = jnp.concatenate([s, jnp.zeros((LX - R * nb, nn * LX), f32)], axis=0)
    s_h, s_l = split(s)
    s = mm(turn_h[...], s_h) + mm(turn_l[...], s_h) + mm(turn_h[...], s_l)
    s = jnp.concatenate([s[:R * nb] * scale, s[R * nb:]], axis=0)
    s_h, s_l = split(s)
    s = mm(unturn_h[...], s_h) + mm(unturn_l[...], s_h) + mm(unturn_h[...], s_l)
    y = mm3(s[:R * nb], back_h[...], back_l[...])
    zsum = jnp.zeros((nd, LX), f32)
    for r in range(R):
        yr = [y[r * nb:(r + 1) * nb, n * LX:(n + 1) * LX] for n in range(nn)]
        back[pl.ds(r, nd, stride=8), :] = jnp.concatenate(yr, axis=0)
        back[pl.ds(R + r, nd, stride=8), :] = jnp.concatenate([behind(a) for a in yr], axis=0)
        mine = (lane >= SLOT * r) & (lane < SLOT * (r + 1))
        ends = jnp.concatenate([qxl * yr[n] - qxf * yr[(n + 1) % nn] for n in range(nn)], axis=0)
        zsum = zsum + jnp.where(mine, mm3(ends, dc_h, dc_l), 0.0)
    zs = blocks(zsum)
    u = coupled([qzl * zs[n] - qzf * behind(zs[n]) for n in range(nn)])
    w = [jnp.where(low_half, t[n] - u[n], 0.0) for n in range(nn)]
    back[pl.ds(2 * R, nd, stride=8), :] = jnp.concatenate(
        [w[n] + pltpu.roll(w[(n - 1) % nn], LZ, 1) for n in range(nn)], axis=0)
    back[pl.ds(2 * R + 1, nd, stride=8), :] = jnp.zeros((nd, LX), f32)
    home = ship(back, got, s2, r2)
    out.wait_send()
    home.wait_recv()
    home.wait_send()


def solve_part(source, to_modes, walls, own):
    nn, nb = lax.axis_size("narrow"), lax.axis_size("wide")
    f32 = jnp.float32
    nd = nn * nb
    edge = np.zeros((LZ, LX, LX))
    for j in range(LZ):
        edge[j, :, j] = QXL
        edge[j, :, LZ + j] = QXF
    edge_h, edge_l = halves(edge.reshape(LZ // 2, 2 * LX, LX))
    slot = np.arange(LX) % LZ
    nu_lane = NU[slot][None]
    table, ex = fourier(nn * LX)
    spec = np.einsum("knx,ix->nik", table.reshape(-1, nn, LX), QX).reshape(nn * LX, nn * LX)
    turn, eb = fourier(nb)
    turn = np.kron(np.eye(LX // nb), turn)
    q_lane = np.zeros((8 + 2 * LX, LX))
    q_lane[0], q_lane[1], q_lane[2], q_lane[3] = QXL, QXF, QZL[slot], QZF[slot]
    q_lane[8:8 + LX] = (QXL ** 2)[:, None]
    q_lane[8 + LX:] = (QXL * QXF)[:, None]
    single = [MU[None], paired(QX.T), np.concatenate([edge_h, edge_l], axis=2), edge_h, nu_lane,
              np.broadcast_to(NU[slot][:, None], (LX, LX)), np.broadcast_to(MU[:, None], (LX, LX)), q_lane,
              *halves(spec), *halves(spec.T), *halves(turn), *halves(turn.T),
              np.broadcast_to(1 - eb[:, None] / 2, (nb, nn * LX)), ex[None]]
    consts = [jnp.asarray(a if a.dtype == ml_dtypes.bfloat16 else a.astype(np.float32)) for a in single]
    vmem, smem = (pl.BlockSpec(memory_space=m) for m in (pltpu.VMEM, pltpu.SMEM))
    dma = pltpu.SemaphoreType.DMA
    return pl.pallas_call(
        functools.partial(solve_kernel, nn, nb),
        out_shape=(jax.ShapeDtypeStruct((LZ, NY, LX), f32), jax.ShapeDtypeStruct((nd * 8, LX), f32)),
        in_specs=[vmem, vmem, vmem, smem] + [vmem] * len(consts),
        out_specs=(vmem, vmem),
        scratch_shapes=[
            pltpu.VMEM((LZ, NY, LX), f32), pltpu.VMEM((LZ, NY, LX), f32), pltpu.VMEM((NY, LX), f32), pltpu.VMEM((NY, LX), f32),
            pltpu.VMEM((nd * 8, LX), f32), pltpu.VMEM((nd * 8, LX), f32), pltpu.VMEM((nd * 8, LX), f32),
            dma, dma, dma, dma, dma,
        ],
        compiler_params=pltpu.CompilerParams(collective_id=1, has_side_effects=True, vmem_limit_bytes=56 * 1024 * 1024),
        name="modes_solve",
    )(source, to_modes, walls, own, *consts)


def last_kernel(fh, got, walls, from_modes, spacing, star_hbm, mu_row, xw, side_x, side_z, out_hbm,
                star, ph, press, across, load_sem, store_sem):
    f32 = jnp.float32
    loads = [pltpu.make_async_copy(star_hbm.at[c], star.at[c], load_sem.at[c]) for c in range(3)]
    for cp in loads:
        cp.start()
    nd = got.shape[0] // 8
    lane = lax.broadcasted_iota(jnp.int32, (nd, LX), 1)
    rim = got[pl.ds(2 * R, nd, stride=8), :]
    cols = []
    for r in range(R):
        a = jnp.where(lane < SLOT, rim if r == 0 else pltpu.roll(rim, LX - SLOT * r, 1), 0.0)
        high = a.astype(jnp.bfloat16).astype(f32)
        low = a - high
        cols.append(high + pltpu.roll(low, SLOT, 1) + pltpu.roll(high, 2 * SLOT, 1))
    cols = jnp.concatenate(cols, axis=0).astype(jnp.bfloat16)
    yb = [got[pl.ds(r, nd, stride=8), :] for r in range(R)]
    ya = [got[pl.ds(R + r, nd, stride=8), :] for r in range(R)]
    for r in range(R):
        across[0, pl.ds(r * nd, nd), :] = yb[r]
        across[1, pl.ds(r * nd, nd), :] = ya[r]
    for j in range(LZ):
        ph[1 + j] = mm(cols, side_x[:, j * LX:(j + 1) * LX])

    def chunk(k, _):
        rows = pl.ds(pl.multiple_of(k * 8, 8), 8)
        b, a = across[0, rows, :], across[1, rows, :]
        jump = (b - a, b + a)
        base = walls[rows, :] + mu_row[...]
        f = [(float(QZL[j]) * jump[j % 2] + (ph[1 + j, rows, :] - fh[j, rows, :])) * pl.reciprocal(base + float(NU[j]))
             for j in range(LZ)]
        x = from_cosines(f)
        for z in range(LZ):
            ph[1 + z, rows, :] = x[z]
        ph[0, rows, :] = x[0] - a
        ph[LZ + 1, rows, :] = x[LZ - 1] + b
        return 0

    lax.fori_loop(0, NY // 8, chunk, 0)
    m_high, m_low = split(from_modes[...])

    def modes(a):
        high, low = split(a)
        return mm(m_high, high) + mm(m_low, high) + mm(m_high, low)

    zero = jnp.zeros((8, LX), f32)
    for z in range(0, LZ + 2, 2):
        pair = []
        for k in range(2):
            high, low = split(ph[z + k])
            both = mm(jnp.concatenate([high, low], axis=1), xw[...])
            pair.append(both[:, :LX] + both[:, LX:])
        both = modes(jnp.concatenate(pair, axis=1))
        for k in range(2):
            press[z + k, pl.ds(0, 8), :] = zero
            press[z + k, pl.ds(8, NY), :] = both[:, k * LX:(k + 1) * LX]
            press[z + k, pl.ds(8 + NY, 8), :] = zero
    across[0] = modes(mm(cols, side_z[...]))
    for cp in loads:
        cp.wait()
    part = 64
    lane = lax.broadcasted_iota(jnp.int32, (part, LX), 1)

    def store(k):
        rows = pl.ds(pl.multiple_of(k * part * LZ, 8), part * LZ)
        return [pltpu.make_async_copy(star.at[c, rows], out_hbm.at[c, rows], store_sem.at[c, k]) for c in range(3)]

    def correct(k, _):
        at = pl.multiple_of(k * part, part)
        rim = across[0, pl.ds(at, part), :]
        slope = 0.05 * spacing[pl.ds(at, part), :]
        for z in range(LZ):
            p = press[1 + z, pl.ds(at + 8, part), :]
            east = jnp.where(lane == LX - 1, p + rim[:, z:z + 1], pltpu.roll(p, LX - 1, 1))
            west = jnp.where(lane == 0, p - rim[:, LZ + z:LZ + z + 1], pltpu.roll(p, 1, 1))
            up = press[1 + z, pl.ds(at + 9, part), :]
            down = press[1 + z, pl.ds(at + 7, part), :]
            north = press[2 + z, pl.ds(at + 8, part), :]
            south = press[z, pl.ds(at + 8, part), :]
            rows = pl.ds(at * LZ + z, part, stride=LZ)
            star[0, rows, :] = star[0, rows, :] - 0.05 * (east - west)
            star[1, rows, :] = star[1, rows, :] - slope * (up - down)
            star[2, rows, :] = star[2, rows, :] - 0.05 * (north - south)
        for cp in store(k):
            cp.start()
        return 0

    lax.fori_loop(0, NY // part, correct, 0)

    def finish(k, _):
        for cp in store(k):
            cp.wait()
        return 0

    lax.fori_loop(0, NY // part, finish, 0)


def last_part(fh, got, walls, from_modes, spacing, star):
    f32 = jnp.float32
    side_x = np.zeros((SLOT, LZ, LX))
    side_z = np.zeros((SLOT, LX))
    for j in range(LZ):
        side_x[j, j] = QXL
        side_x[LZ + j, j] = -QXF
    side_z[:LZ, :LZ] = QZ
    side_z[LZ:, LZ:SLOT] = QZ

    def stacked(a):
        high, low = halves(a)
        return jnp.asarray(np.concatenate([high, high, low, np.zeros_like(low)], axis=0))

    consts = [jnp.asarray(MU[None].astype(np.float32)), jnp.asarray(paired(QX)),
              stacked(side_x.reshape(SLOT, LZ * LX)), stacked(side_z)]
    vmem, any_ = (pl.BlockSpec(memory_space=m) for m in (pltpu.VMEM, pl.ANY))
    parts = NY // 64
    return pl.pallas_call(
        last_kernel,
        out_shape=jax.ShapeDtypeStruct((3, ROWS, LX), f32),
        in_specs=[vmem] * 5 + [any_] + [vmem] * 4,
        out_specs=any_,
        scratch_shapes=[
            pltpu.VMEM((3, ROWS, LX), f32), pltpu.VMEM((LZ + 2, NY, LX), f32), pltpu.VMEM((LZ + 2, NY + 16, LX), f32),
            pltpu.VMEM((2, NY, LX), f32), pltpu.SemaphoreType.DMA((3,)), pltpu.SemaphoreType.DMA((3, parts)),
        ],
        compiler_params=pltpu.CompilerParams(vmem_limit_bytes=56 * 1024 * 1024),
        name="synthesis_correct",
    )(fh, got, walls, from_modes, spacing, star, *consts)


def shards(velocity, inv_spacing, eigen_wall, to_modes, from_modes):
    star, source, walls = first_part(velocity, inv_spacing, eigen_wall)
    nn, nb = lax.axis_size("narrow"), lax.axis_size("wide")
    c_all = walls[:, 0, :3].reshape(nb, nn, 3).transpose(1, 0, 2).reshape(-1)
    me = lax.axis_index("narrow") * nb + lax.axis_index("wide")
    own = lax.dynamic_index_in_dim(c_all.reshape(-1, nn * nb), me, axis=1, keepdims=False)
    spread = jnp.broadcast_to(c_all[:, None], (NY, LX))
    fh, got = solve_part(source, to_modes, spread, own)
    spacing = jnp.broadcast_to(inv_spacing[:, None], (NY, LX))
    return last_part(fh, got, spread, from_modes, spacing, star).reshape(3, NY, LZ, LX)


def solution(mesh):
    in_specs = (P(None, None, "wide", "narrow"), P(), P(("narrow", "wide")), P(), P())
    out_specs = P(None, None, "wide", "narrow")
    return jax.shard_map(shards, mesh=mesh, in_specs=in_specs, out_specs=out_specs, check_vma=False)
```

profile of v0, /device:TPU:1, one launch (start us, length us, event | category | flops | bytes accessed | tf_op | source)
XLA Modules:
  0.0 139.6 jit_solution(11681921231646503049)
XLA Ops:
  0.0 1.5 %broadcast_in_dim.15.spacing = f32[384,128]{1,0:T(8,128)} broadcast(f32[384]{0:T(512)} %spacing.1), dimensions={0} | broadcast | bytes 198144 | tf_op jit(solution)/shard_map/broadcast_in_dim | solution.py:648
  1.5 74.2 %predict_diverge.1 = (f32[3,6144,128]{2,1,0:T(8,128)}, f32[16,384,128]{2,1,0:T(8,128)}, f32[128,1,128]{2,1,0:T(1,128)}) custom-call(f32[3,6144,128]{2,1,0:T(8,128)} %bitcast.7, f32[384]{0:T(512)} %spacing.1, f32[3]{0:T(128)} %eig.1), custom_call_target="tpu_custom_call" | custom-call | tf_op jit(solution)/shard_map/predict_diverge/pallas_call | solution.py:220
  75.7 0.8 copy.31
  76.5 0.2 reshape_reshape.3
  76.7 0.2 broadcast_in_dim.6
  76.9 0.7 dynamic-slice_reduce_fusion.own
  77.6 0.8 broadcast_in_dim.14.walls
  78.4 40.3 %modes_solve.1 = (f32[16,384,128]{2,1,0:T(8,128)}, f32[1024,128]{1,0:T(8,128)}) custom-call(f32[16,384,128]{2,1,0:T(8,128)} %get-tuple-element.10.source, f32[384,384]{1,0:T(8,128)} %to_modes.1, f32[384,128]{1,0:T(8,128)} %broadcast_in_dim.14.walls, f32[3]{0:T(128)} %dynamic-slice_reduce_fusion.own, f32[1,128]{1,0:T(1,128)} %constant.59.clone.mu_row, ...), custom_call_target="tpu_custom_call" | custom-call | tf_op jit(solution)/shard_map/modes_solve/pallas_call | solution.py:496
  118.7 20.7 %synthesis_correct.1 = f32[3,6144,128]{2,1,0:T(8,128)} custom-call(f32[16,384,128]{2,1,0:T(8,128)} %get-tuple-element.12.fh, f32[1024,128]{1,0:T(8,128)} %get-tuple-element.13.got, f32[384,128]{1,0:T(8,128)} %broadcast_in_dim.14.walls, f32[384,384]{1,0:T(8,128)} %from_modes.1, f32[384,128]{1,0:T(8,128)} %broadcast_in_dim.15.spacing, ...), custom_call_target="tpu_custom_call" | custom-call | tf_op jit(solution)/shard_map/synthesis_correct/pallas_call | solution.py:626
where the time goes:
time: 140 us
  Pallas kernels  135 us (96%)
  local copies, waits for them, and re-layouts  4.22 us (3%)
    pallas_call x1, Pallas kernels, first_part(): pl.pallas_call(functools.partial(first_kernel, nn, nb), out_shape=(jax.Sh...  74.2 us
    pallas_call x1, Pallas kernels, solve_part(): pl.pallas_call(functools.partial(solve_kernel, nn, nb), out_shape=(jax.Sh...  40.3 us
    pallas_call x1, Pallas kernels, last_part(): pl.pallas_call(last_kernel, out_shape=jax.ShapeDtypeStruct((3, ROWS, LX),...  20.7 us

commit v1 on v0

--- a/solution.py
+++ b/solution.py
@@ -18,9 +18,92 @@
 GROUPS = NY // LX
 
 
-def first_kernel(nn, nb, v_hbm, spacing, eig, star_hbm, source, walls,
-                 v, star, src, zsend, zrecv, xsend, xrecv, s2send, s2recv, x0send, x0recv,
-                 load_sem, store_sem, z_ss, z_rs, x_ss, x_rs, s2_ss, s2_rs, x0_ss, x0_rs, e_ss, e_rs):
+def split(a):
+    high = a.astype(jnp.bfloat16)
+    return high, (a - high.astype(jnp.float32)).astype(jnp.bfloat16)
+
+
+def mm(a, b):
+    return jnp.dot(a, b, preferred_element_type=jnp.float32)
+
+
+def mm3(a, b_high, b_low):
+    high, low = split(a)
+    return mm(high, b_high) + mm(low, b_high) + mm(high, b_low)
+
+
+def cosines(n):
+    j = np.arange(n)[:, None]
+    z = np.arange(n)[None, :]
+    q = np.cos(np.pi * j * (z + 0.5) / n) * np.where(j == 0, math.sqrt(1 / n), math.sqrt(2 / n))
+    return q, 2 - 2 * np.cos(np.pi * np.arange(n) / n)
+
+
+def fourier(n):
+    r = np.arange(n)[:, None]
+    c = np.arange(n)[None, :]
+    mid = n // 2
+    k = np.where(r <= mid, r, r - mid)
+    phase = (k * c % n) * (2 * np.pi / n)
+    waves = np.where(r <= mid, np.cos(phase), np.sin(phase))
+    weight = np.where((r == 0) | (r == mid), math.sqrt(1 / n), math.sqrt(2 / n))
+    return waves * weight, 2 - 2 * np.cos(2 * np.pi * k[:, 0] / n)
+
+
+def halves(a):
+    a = np.asarray(a, np.float32)
+    high = a.astype(ml_dtypes.bfloat16)
+    return high, (a - high.astype(np.float32)).astype(ml_dtypes.bfloat16)
+
+
+def paired(a):
+    high, low = halves(a)
+    return np.block([[high, low], [high, np.zeros_like(low)]])
+
+
+QZ, NU = cosines(LZ)
+QX, MU = cosines(LX)
+QZL, QZF = QZ[:, -1], QZ[:, 0]
+QXL, QXF = QX[:, -1], QX[:, 0]
+SLOT = 2 * LZ
+R = 3
+
+
+def to_cosines(x):
+    n = len(x)
+    out = [None] * n
+    e = [x[z] + x[n - 1 - z] for z in range(n // 2)]
+    o = [x[z] - x[n - 1 - z] for z in range(n // 2)]
+    ee = [e[z] + e[n // 2 - 1 - z] for z in range(n // 4)]
+    eo = [e[z] - e[n // 2 - 1 - z] for z in range(n // 4)]
+    for j in range(n):
+        part = o if j % 2 else (eo if j % 4 else ee)
+        out[j] = sum(float(QZ[j, z]) * part[z] for z in range(len(part)))
+    return out
+
+
+def from_cosines(f):
+    n = len(f)
+    even, out = [None] * (n // 2), [None] * n
+    for z in range(n // 4):
+        a = sum(float(QZ[j, z]) * f[j] for j in range(0, n, 4))
+        b = sum(float(QZ[j, z]) * f[j] for j in range(2, n, 4))
+        even[z], even[n // 2 - 1 - z] = a + b, a - b
+    for z in range(n // 2):
+        odd = sum(float(QZ[j, z]) * f[j] for j in range(1, n, 2))
+        out[z], out[n - 1 - z] = even[z] + odd, even[z] - odd
+    return out
+
+
+def front_kernel(nn, nb, v_hbm, spacing, eig, modes_hbm, xw_hbm, edge_hl_hbm, edge_h_hbm, spec_h_hbm, spec_l_hbm,
+                 back_h_hbm, back_l_hbm, mu_row, nu_lane, nu_row, mu_col, q_lane, turn_h, turn_l, unturn_h, unturn_l,
+                 cos_b, ex_row, star_hbm, walls, fh, got,
+                 v, star, rim, zsend, zrecv, xsend, xrecv, s2send, s2recv, x0send, x0recv,
+                 load_sem, store_sem, z_ss, z_rs, x_ss, x_rs, s2_ss, s2_rs, x0_ss, x0_rs, e_ss, e_rs,
+                 source, tiles, gz, gh, zl, zf, send, recv, back, s1, r1, s2, r2,
+                 to_modes, xw, edge_hl, edge_h, spec_h, spec_l, back_h, back_l, const_sem):
+    large = ((modes_hbm, to_modes), (xw_hbm, xw), (edge_hl_hbm, edge_hl), (edge_h_hbm, edge_h),
+             (spec_h_hbm, spec_h), (spec_l_hbm, spec_l), (back_h_hbm, back_h), (back_l_hbm, back_l))
     me_n = lax.axis_index("narrow")
     me_b = lax.axis_index("wide")
     ring = nb // 4
@@ -35,6 +118,9 @@
     for c in (2, 0, 1):
         loads[c].start()
 
+    fetches = [pltpu.make_async_copy(h, m, const_sem.at[k]) for k, (h, m) in enumerate(large)]
+    for cp in fetches:
+        cp.start()
     barrier = pltpu.get_barrier_semaphore()
     narrow_peers = [(lax.rem(me_n + k, nn), me_b) for k in range(1, nn)]
     spot_peers = [(me_n, layer * ring + lax.rem(spot + k, ring)) for k in range(1, ring)]
@@ -49,22 +135,25 @@
         v[c, pl.ds(LZ + ROWS, LZ), :] = zero
         star[c, pl.ds(0, LZ), :] = zero
         star[c, pl.ds(LZ + ROWS, LZ), :] = zero
-    lane1 = lax.broadcasted_iota(jnp.int32, (1, LX), 1)
-    row = jnp.where(lane1 == 0, eig[0], jnp.where(lane1 == 1, eig[1], jnp.where(lane1 == 2, eig[2], 0.0)))
-    my_wall = me_b * nn + me_n
-    walls[my_wall] = row
+    each = NY // (nn * nb)
+    me = me_n * nb + me_b
+    which = lax.broadcasted_iota(jnp.int32, (8, LX), 0)
+    values = jnp.zeros((8, LX), jnp.float32)
+    for k in range(each):
+        values = jnp.where(which == k, eig[k], values)
+    tiles[pl.ds(pl.multiple_of(me * 8, 8), 8), :] = values
     pl.semaphore_wait(barrier, len(greeted))
 
     def share(peers, at, count, stage):
         for k, peer in enumerate(peers):
             pltpu.make_async_remote_copy(
-                src_ref=walls.at[pl.ds(at, count)], dst_ref=walls.at[pl.ds(at, count)],
+                src_ref=tiles.at[pl.ds(pl.multiple_of(at * 8, 8), count * 8)], dst_ref=tiles.at[pl.ds(pl.multiple_of(at * 8, 8), count * 8)],
                 send_sem=e_ss.at[stage], recv_sem=e_rs.at[stage], device_id=peer, device_id_type=MESH).start()
 
     def share_wait(peers, count, stage):
         n = len(peers) * count
         w = pltpu.make_async_remote_copy(
-            src_ref=walls.at[pl.ds(0, n)], dst_ref=walls.at[pl.ds(0, n)],
+            src_ref=tiles.at[pl.ds(0, n * 8)], dst_ref=tiles.at[pl.ds(0, n * 8)],
             send_sem=e_ss.at[stage], recv_sem=e_rs.at[stage], device_id=peers[0], device_id_type=MESH)
         w.wait_send()
         w.wait_recv()
@@ -84,10 +173,10 @@
             last = jnp.where(lane == yy, turned, last)
             first = jnp.where(lane == lax.rem(yy + 1, LX), turned, first)
             return last, first
-        last, first = lax.fori_loop(0, LX, step, (zero, zero), unroll=8)
+        last, first = lax.fori_loop(0, LX, step, (zero, zero), unroll=16)
         return last, pltpu.roll(first, LX - 1, 1)
 
-    share(narrow_peers, my_wall, 1, 0)
+    share(spot_peers, me, 1, 0)
     zcopies, xcopies = [], []
     for c in (2, 0, 1):
         loads[c].wait()
@@ -106,12 +195,21 @@
             cp.start()
             xcopies.append(cp)
 
-    share_wait(narrow_peers, 1, 0)
-    share(spot_peers, me_b * nn, nn, 1)
+    share_wait(spot_peers, 1, 0)
+    share(layer_peers, me_n * nb + layer * ring, ring, 1)
     for cp in xcopies:
         cp.wait_recv()
-
-    def predict_plane(y, _):
+    even = lax.rem(lane, 2) == 0
+
+    def interleave(east, west):
+        west = pltpu.roll(west, 1, 1)
+        return jnp.where(even, east, west), jnp.where(even, west, east)
+
+    for c in range(3):
+        for g in range(GROUPS):
+            rim[c, g, 0], rim[c, g, 1] = interleave(xrecv[1, c, g], xrecv[0, c, g])
+
+    def predict_plane(y, odd):
         g = y // LX
         yy = lax.rem(y, LX)
         base = pl.multiple_of(LZ + y * LZ, LZ)
@@ -126,24 +224,27 @@
         a_u = curve - slope
         a_l = curve + slope
         a_c = 0.8 - 2.0 * curve
-        to_last = lax.rem(2 * LX - 1 - yy, LX)
-        to_first = lax.rem(LX - yy, LX)
         for c in range(3):
             f = centre[c]
             upper = v[c, pl.ds(base + LZ, LZ), :]
             lower = v[c, pl.ds(base - LZ, LZ), :]
-            north = pltpu.roll(f, LZ - 1, 0)
-            south = pltpu.roll(f, 1, 0)
-            east = jnp.where(lane == LX - 1, pltpu.roll(xrecv[1, c, g], to_last, 1), pltpu.roll(f, LX - 1, 1))
-            west = jnp.where(lane == 0, pltpu.roll(xrecv[0, c, g], to_first, 1), pltpu.roll(f, 1, 1))
+            north = v[c, pl.ds(base + 1, LZ), :]
+            south = v[c, pl.ds(base - 1, LZ), :]
+            ends = pltpu.roll(rim[c, g, odd], LX - 1 - yy, 1)
+            east = jnp.where(lane == LX - 1, ends, pltpu.roll(f, LX - 1, 1))
+            west = jnp.where(lane == 0, ends, pltpu.roll(f, 1, 1))
             star[c, pl.ds(base, LZ), :] = (
                 a_c * f + a_e * east + a_w * west + (a_n * north + a_s * south) + (a_u * upper + a_l * lower))
+
+    def predict_pair(k, _):
+        predict_plane(2 * k, 0)
+        predict_plane(2 * k + 1, 1)
         return 0
 
-    lax.fori_loop(0, NY, predict_plane, 0, unroll=2)
-
-    share_wait(spot_peers, nn, 1)
-    share(layer_peers, layer * ring * nn, ring * nn, 2)
+    lax.fori_loop(0, NY // 2, predict_pair, 0, unroll=8)
+
+    share_wait(layer_peers, ring, 1)
+    share(narrow_peers, me_n * nb, nb, 2)
     for cp in zcopies:
         cp.wait_recv()
     part = 96
@@ -180,165 +281,56 @@
         cp.start()
     for cp in x0copies:
         cp.wait_recv()
-
-    def diverge_plane(y, _):
+    for g in range(GROUPS):
+        rim[0, g, 0], rim[0, g, 1] = interleave(x0recv[1, g], x0recv[0, g])
+
+    def diverge_plane(y, odd):
         g = y // LX
         yy = lax.rem(y, LX)
         base = pl.multiple_of(LZ + y * LZ, LZ)
         s = 5.0 * spacing[y]
-        to_last = lax.rem(2 * LX - 1 - yy, LX)
-        to_first = lax.rem(LX - yy, LX)
         f = star[0, pl.ds(base, LZ), :]
-        east = jnp.where(lane == LX - 1, pltpu.roll(x0recv[1, g], to_last, 1), pltpu.roll(f, LX - 1, 1))
-        west = jnp.where(lane == 0, pltpu.roll(x0recv[0, g], to_first, 1), pltpu.roll(f, 1, 1))
-        h = star[2, pl.ds(base, LZ), :]
-        north = jnp.where(level == LZ - 1, 0.0, pltpu.roll(h, LZ - 1, 0))
-        south = jnp.where(level == 0, 0.0, pltpu.roll(h, 1, 0))
+        ends = pltpu.roll(rim[0, g, odd], LX - 1 - yy, 1)
+        east = jnp.where(lane == LX - 1, ends, pltpu.roll(f, LX - 1, 1))
+        west = jnp.where(lane == 0, ends, pltpu.roll(f, 1, 1))
+        north = jnp.where(level == LZ - 1, 0.0, star[2, pl.ds(base + 1, LZ), :])
+        south = jnp.where(level == 0, 0.0, star[2, pl.ds(base - 1, LZ), :])
         rise = star[1, pl.ds(base + LZ, LZ), :] - star[1, pl.ds(base - LZ, LZ), :]
-        src[pl.ds(pl.multiple_of(y * LZ, LZ), LZ), :] = 5.0 * ((east - west) + (north - south)) + s * rise
+        source[pl.ds(y, LZ, stride=NY), :] = 5.0 * ((east - west) + (north - south)) + s * rise
+
+    def diverge_pair(k, _):
+        diverge_plane(2 * k, 0)
+        diverge_plane(2 * k + 1, 1)
         return 0
 
-    lax.fori_loop(0, NY, diverge_plane, 0, unroll=4)
-    for z in range(1, LZ - 1):
-        source[z] = src[pl.ds(z, NY, stride=LZ), :]
+    lax.fori_loop(0, NY // 2, diverge_pair, 0, unroll=8)
+
+    f32 = jnp.float32
+    nd = nn * nb
+    for cp in fetches:
+        cp.wait()
+    t_high, t_low = split(to_modes[...])
+
+    def slabs(pair):
+        s_high, s_low = split(jnp.concatenate([source[pl.ds(z * NY, NY), :] for z in pair], axis=1))
+        modal = mm(t_high, s_high) + mm(t_low, s_high) + mm(t_high, s_low)
+        for k, z in enumerate(pair):
+            high, low = split(modal[:, k * LX:(k + 1) * LX])
+            both = mm(jnp.concatenate([high, low], axis=1), xw[...])
+            gz[z] = both[:, :LX] + both[:, LX:]
+
+    for z in range(1, LZ - 1, 2):
+        slabs((z, z + 1))
     for cp in s2copies:
         cp.wait_recv()
-    source[0] = src[pl.ds(0, NY, stride=LZ), :] - 5.0 * s2recv[0]
-    source[LZ - 1] = src[pl.ds(LZ - 1, NY, stride=LZ), :] + 5.0 * s2recv[1]
-    share_wait(layer_peers, ring * nn, 2)
-    for cp in zcopies + xcopies + s2copies + x0copies:
-        cp.wait_send()
-    for cp in stores:
-        cp.wait()
-
-
-def first_part(velocity, inv_spacing, eigen_wall):
-    nn, nb = lax.axis_size("narrow"), lax.axis_size("wide")
-    f32 = jnp.float32
-    any_, vmem, smem = (pl.BlockSpec(memory_space=m) for m in (pl.ANY, pltpu.VMEM, pltpu.SMEM))
-    dma = pltpu.SemaphoreType.DMA
-    return pl.pallas_call(
-        functools.partial(first_kernel, nn, nb),
-        out_shape=(jax.ShapeDtypeStruct((3, ROWS, LX), f32), jax.ShapeDtypeStruct((LZ, NY, LX), f32),
-                   jax.ShapeDtypeStruct((nn * nb, 1, LX), f32)),
-        in_specs=[any_, smem, smem],
-        out_specs=(any_, vmem, vmem),
-        scratch_shapes=[
-            pltpu.VMEM((3, ROWS + 2 * LZ, LX), f32), pltpu.VMEM((3, ROWS + 2 * LZ, LX), f32), pltpu.VMEM((ROWS, LX), f32),
-            pltpu.VMEM((2, 3, NY, LX), f32), pltpu.VMEM((2, 3, NY, LX), f32),
-            pltpu.VMEM((2, 3, GROUPS, LZ, LX), f32), pltpu.VMEM((2, 3, GROUPS, LZ, LX), f32),
-            pltpu.VMEM((2, NY, LX), f32), pltpu.VMEM((2, NY, LX), f32),
-            pltpu.VMEM((2, GROUPS, LZ, LX), f32), pltpu.VMEM((2, GROUPS, LZ, LX), f32),
-            dma((3,)), dma((3,)), dma((2, 3)), dma((2, 3)), dma((2, 3)), dma((2, 3)),
-            dma((2,)), dma((2,)), dma((2,)), dma((2,)), dma((3,)), dma((3,)),
-        ],
-        compiler_params=pltpu.CompilerParams(collective_id=0, has_side_effects=True, vmem_limit_bytes=56 * 1024 * 1024),
-        name="predict_diverge",
-    )(velocity.reshape(3, ROWS, LX), inv_spacing, eigen_wall)
-
-
-def split(a):
-    high = a.astype(jnp.bfloat16)
-    return high, (a - high.astype(jnp.float32)).astype(jnp.bfloat16)
-
-
-def mm(a, b):
-    return jnp.dot(a, b, preferred_element_type=jnp.float32)
-
-
-def mm3(a, b_high, b_low):
-    high, low = split(a)
-    return mm(high, b_high) + mm(low, b_high) + mm(high, b_low)
-
-
-def cosines(n):
-    j = np.arange(n)[:, None]
-    z = np.arange(n)[None, :]
-    q = np.cos(np.pi * j * (z + 0.5) / n) * np.where(j == 0, math.sqrt(1 / n), math.sqrt(2 / n))
-    return q, 2 - 2 * np.cos(np.pi * np.arange(n) / n)
-
-
-def fourier(n):
-    r = np.arange(n)[:, None]
-    c = np.arange(n)[None, :]
-    mid = n // 2
-    k = np.where(r <= mid, r, r - mid)
-    phase = (k * c % n) * (2 * np.pi / n)
-    waves = np.where(r <= mid, np.cos(phase), np.sin(phase))
-    weight = np.where((r == 0) | (r == mid), math.sqrt(1 / n), math.sqrt(2 / n))
-    return waves * weight, 2 - 2 * np.cos(2 * np.pi * k[:, 0] / n)
-
-
-def halves(a):
-    a = np.asarray(a, np.float32)
-    high = a.astype(ml_dtypes.bfloat16)
-    return high, (a - high.astype(np.float32)).astype(ml_dtypes.bfloat16)
-
-
-def paired(a):
-    high, low = halves(a)
-    return np.block([[high, low], [high, np.zeros_like(low)]])
-
-
-QZ, NU = cosines(LZ)
-QX, MU = cosines(LX)
-QZL, QZF = QZ[:, -1], QZ[:, 0]
-QXL, QXF = QX[:, -1], QX[:, 0]
-SLOT = 2 * LZ
-R = 3
-
-
-def to_cosines(x):
-    n = len(x)
-    out = [None] * n
-    e = [x[z] + x[n - 1 - z] for z in range(n // 2)]
-    o = [x[z] - x[n - 1 - z] for z in range(n // 2)]
-    ee = [e[z] + e[n // 2 - 1 - z] for z in range(n // 4)]
-    eo = [e[z] - e[n // 2 - 1 - z] for z in range(n // 4)]
-    for j in range(n):
-        part = o if j % 2 else (eo if j % 4 else ee)
-        out[j] = sum(float(QZ[j, z]) * part[z] for z in range(len(part)))
-    return out
-
-
-def from_cosines(f):
-    n = len(f)
-    even, out = [None] * (n // 2), [None] * n
-    for z in range(n // 4):
-        a = sum(float(QZ[j, z]) * f[j] for j in range(0, n, 4))
-        b = sum(float(QZ[j, z]) * f[j] for j in range(2, n, 4))
-        even[z], even[n // 2 - 1 - z] = a + b, a - b
-    for z in range(n // 2):
-        odd = sum(float(QZ[j, z]) * f[j] for j in range(1, n, 2))
-        out[z], out[n - 1 - z] = even[z] + odd, even[z] - odd
-    return out
-
-
-def solve_kernel(nn, nb, source, to_modes, walls, own, mu_row, xw, edge_hl, edge_h, nu_lane, nu_row, mu_col, q_lane,
-                 spec_h, spec_l, back_h, back_l, turn_h, turn_l, unturn_h, unturn_l, cos_b, ex_row,
-                 fh, got, gz, gh, zl, zf, send, recv, back, s1, r1, s2, r2, loc):
-    f32 = jnp.float32
-    nd = nn * nb
-    me_n = lax.axis_index("narrow")
-    me_b = lax.axis_index("wide")
-    me = me_n * nb + me_b
-    barrier = pltpu.get_barrier_semaphore()
-
-    def greet(k, _):
-        d = lax.rem(me + k, nd)
-        pl.semaphore_signal(barrier, inc=1, device_id=(d // nb, lax.rem(d, nb)), device_id_type=MESH)
-        return 0
-
-    lax.fori_loop(1, nd, greet, 0)
-
-    t_high, t_low = split(to_modes[...])
-    for z in range(0, LZ, 2):
-        s_high, s_low = split(jnp.concatenate([source[z], source[z + 1]], axis=1))
-        modal = mm(t_high, s_high) + mm(t_low, s_high) + mm(t_high, s_low)
-        for k in range(2):
-            high, low = split(modal[:, k * LX:(k + 1) * LX])
-            both = mm(jnp.concatenate([high, low], axis=1), xw[...])
-            gz[z + k] = both[:, :LX] + both[:, LX:]
+    low, top = pl.ds(0, NY), pl.ds((LZ - 1) * NY, NY)
+    source[low, :] = source[low, :] - 5.0 * s2recv[0]
+    source[top, :] = source[top, :] + 5.0 * s2recv[1]
+    slabs((0, LZ - 1))
+    share_wait(narrow_peers, nb, 2)
+    each = NY // nd
+    for k in range(each):
+        walls[pl.ds(k, nd, stride=each), :] = tiles[pl.ds(k, nd, stride=8), :]
 
     def chunk(k, _):
         rows = pl.ds(pl.multiple_of(k * 8, 8), 8)
@@ -370,16 +362,16 @@
             packed = packed + pltpu.roll(edge[r * nd:(r + 1) * nd], SLOT * r, 1)
     send[pl.ds(2 * R, nd, stride=8), :] = packed
     send[pl.ds(2 * R + 1, nd, stride=8), :] = jnp.zeros((nd, LX), f32)
-    pl.semaphore_wait(barrier, nd - 1)
 
     def ship(src, dst, ss, rs):
         def go(k, _):
-            d = lax.rem(me + k, nd)
+            d = me + k
+            d = jnp.where(d >= nd, d - nd, d)
             pltpu.make_async_remote_copy(
                 src_ref=src.at[pl.ds(pl.multiple_of(d * 8, 8), 8)], dst_ref=dst.at[pl.ds(pl.multiple_of(me * 8, 8), 8)],
-                send_sem=ss, recv_sem=rs, device_id=(d // nb, lax.rem(d, nb)), device_id_type=MESH).start()
+                send_sem=ss, recv_sem=rs, device_id=d, device_id_type=pl.DeviceIdType.LOGICAL).start()
             return 0
-        lax.fori_loop(1, nd, go, 0)
+        lax.fori_loop(1, nd, go, 0, unroll=8)
         mine = pl.ds(pl.multiple_of(me * 8, 8), 8)
         dst[mine, :] = src[mine, :]
         most = pl.ds(0, (nd - 1) * 8)
@@ -388,6 +380,7 @@
 
     out = ship(send, recv, s1, r1)
 
+    own = [walls[pl.ds(r * nd + me, 1), :] for r in range(R)]
     lane = lax.broadcasted_iota(jnp.int32, (1, LX), 1)
     owner_lane = jnp.where(lane < SLOT, own[0], jnp.where(lane < 2 * SLOT, own[1], own[2]))
     rowid = lax.broadcasted_iota(jnp.int32, (LX, LX), 0)
@@ -408,8 +401,9 @@
     for r in range(R):
         gll = jnp.zeros_like(ex_row[...])
         glf = jnp.zeros_like(ex_row[...])
+        base = jnp.concatenate([own[r]] * nn, axis=1) + ex_row[...]
         for j in range(LZ):
-            g = 1.0 / (own[r] + float(NU[j]) + ex_row[...])
+            g = 1.0 / (base + float(NU[j]))
             gll = gll + float(QZL[j] ** 2) * g
             glf = glf + float(QZL[j] * QZF[j]) * g
         scale.append(1.0 / (1 + 2 * gll - 2 * glf * cos_b[...]))
@@ -465,9 +459,13 @@
     out.wait_send()
     home.wait_recv()
     home.wait_send()
-
-
-def solve_part(source, to_modes, walls, own):
+    for cp in zcopies + xcopies + s2copies + x0copies:
+        cp.wait_send()
+    for cp in stores:
+        cp.wait()
+
+
+def front_part(velocity, inv_spacing, eigen_wall, to_modes):
     nn, nb = lax.axis_size("narrow"), lax.axis_size("wide")
     f32 = jnp.float32
     nd = nn * nb
@@ -486,26 +484,35 @@
     q_lane[0], q_lane[1], q_lane[2], q_lane[3] = QXL, QXF, QZL[slot], QZF[slot]
     q_lane[8:8 + LX] = (QXL ** 2)[:, None]
     q_lane[8 + LX:] = (QXL * QXF)[:, None]
-    single = [MU[None], paired(QX.T), np.concatenate([edge_h, edge_l], axis=2), edge_h, nu_lane,
-              np.broadcast_to(NU[slot][:, None], (LX, LX)), np.broadcast_to(MU[:, None], (LX, LX)), q_lane,
-              *halves(spec), *halves(spec.T), *halves(turn), *halves(turn.T),
-              np.broadcast_to(1 - eb[:, None] / 2, (nb, nn * LX)), ex[None]]
-    consts = [jnp.asarray(a if a.dtype == ml_dtypes.bfloat16 else a.astype(np.float32)) for a in single]
-    vmem, smem = (pl.BlockSpec(memory_space=m) for m in (pltpu.VMEM, pltpu.SMEM))
+    big = [paired(QX.T), np.concatenate([edge_h, edge_l], axis=2), edge_h, *halves(spec), *halves(spec.T)]
+    small = [MU[None], nu_lane, np.broadcast_to(NU[slot][:, None], (LX, LX)), np.broadcast_to(MU[:, None], (LX, LX)), q_lane,
+             *halves(turn), *halves(turn.T), np.broadcast_to(1 - eb[:, None] / 2, (nb, nn * LX)), ex[None]]
+    consts = [jnp.asarray(a if a.dtype == ml_dtypes.bfloat16 else a.astype(np.float32)) for a in big + small]
+    any_, vmem, smem = (pl.BlockSpec(memory_space=m) for m in (pl.ANY, pltpu.VMEM, pltpu.SMEM))
     dma = pltpu.SemaphoreType.DMA
     return pl.pallas_call(
-        functools.partial(solve_kernel, nn, nb),
-        out_shape=(jax.ShapeDtypeStruct((LZ, NY, LX), f32), jax.ShapeDtypeStruct((nd * 8, LX), f32)),
-        in_specs=[vmem, vmem, vmem, smem] + [vmem] * len(consts),
-        out_specs=(vmem, vmem),
+        functools.partial(front_kernel, nn, nb),
+        out_shape=(jax.ShapeDtypeStruct((3, ROWS, LX), f32), jax.ShapeDtypeStruct((NY, LX), f32),
+                   jax.ShapeDtypeStruct((LZ, NY, LX), f32), jax.ShapeDtypeStruct((nd * 8, LX), f32)),
+        in_specs=[any_, smem, smem] + [any_] * (1 + len(big)) + [vmem] * len(small),
+        out_specs=(any_, vmem, vmem, vmem),
         scratch_shapes=[
+            pltpu.VMEM((3, ROWS + 2 * LZ, LX), f32), pltpu.VMEM((3, ROWS + 2 * LZ, LX), f32), pltpu.VMEM((3, GROUPS, 2, LZ, LX), f32),
+            pltpu.VMEM((2, 3, NY, LX), f32), pltpu.VMEM((2, 3, NY, LX), f32),
+            pltpu.VMEM((2, 3, GROUPS, LZ, LX), f32), pltpu.VMEM((2, 3, GROUPS, LZ, LX), f32),
+            pltpu.VMEM((2, NY, LX), f32), pltpu.VMEM((2, NY, LX), f32),
+            pltpu.VMEM((2, GROUPS, LZ, LX), f32), pltpu.VMEM((2, GROUPS, LZ, LX), f32),
+            dma((3,)), dma((3,)), dma((2, 3)), dma((2, 3)), dma((2, 3)), dma((2, 3)),
+            dma((2,)), dma((2,)), dma((2,)), dma((2,)), dma((3,)), dma((3,)),
+            pltpu.VMEM((LZ * NY, LX), f32), pltpu.VMEM((nd * 8, LX), f32),
             pltpu.VMEM((LZ, NY, LX), f32), pltpu.VMEM((LZ, NY, LX), f32), pltpu.VMEM((NY, LX), f32), pltpu.VMEM((NY, LX), f32),
             pltpu.VMEM((nd * 8, LX), f32), pltpu.VMEM((nd * 8, LX), f32), pltpu.VMEM((nd * 8, LX), f32),
-            dma, dma, dma, dma, dma,
+            dma, dma, dma, dma,
+            pltpu.VMEM((NY, NY), f32), *[pltpu.VMEM(a.shape, jnp.bfloat16) for a in big], dma((1 + len(big),)),
         ],
-        compiler_params=pltpu.CompilerParams(collective_id=1, has_side_effects=True, vmem_limit_bytes=56 * 1024 * 1024),
-        name="modes_solve",
-    )(source, to_modes, walls, own, *consts)
+        compiler_params=pltpu.CompilerParams(collective_id=0, has_side_effects=True, vmem_limit_bytes=60 * 1024 * 1024),
+        name="predict_solve",
+    )(velocity.reshape(3, ROWS, LX), inv_spacing, eigen_wall, to_modes, *consts)
 
 
 def last_kernel(fh, got, walls, from_modes, spacing, star_hbm, mu_row, xw, side_x, side_z, out_hbm,
@@ -638,15 +645,9 @@
 
 
 def shards(velocity, inv_spacing, eigen_wall, to_modes, from_modes):
-    star, source, walls = first_part(velocity, inv_spacing, eigen_wall)
-    nn, nb = lax.axis_size("narrow"), lax.axis_size("wide")
-    c_all = walls[:, 0, :3].reshape(nb, nn, 3).transpose(1, 0, 2).reshape(-1)
-    me = lax.axis_index("narrow") * nb + lax.axis_index("wide")
-    own = lax.dynamic_index_in_dim(c_all.reshape(-1, nn * nb), me, axis=1, keepdims=False)
-    spread = jnp.broadcast_to(c_all[:, None], (NY, LX))
-    fh, got = solve_part(source, to_modes, spread, own)
+    star, walls, fh, got = front_part(velocity, inv_spacing, eigen_wall, to_modes)
     spacing = jnp.broadcast_to(inv_spacing[:, None], (NY, LX))
-    return last_part(fh, got, spread, from_modes, spacing, star).reshape(3, NY, LZ, LX)
+    return last_part(fh, got, walls, from_modes, spacing, star).reshape(3, NY, LZ, LX)
 
 
 def solution(mesh):

time: 140 us -> 112 us (0.80)
  Pallas kernels: 135 us -> 110 us
  local copies, waits for them, and re-layouts: 4.22 us -> 1.48 us
    pallas_call x2 -> x1, Pallas kernels: 114 us -> 88.9 us  [front_part(): pl.pallas_call(functools.partial(front_kernel, nn, nb), out_shape=(jax.Sh...]
where the time goes in v1:
time: 112 us; the launch traced here: 111 us
  Pallas kernels  110 us (98%)
  local copies, waits for them, and re-layouts  1.48 us (1%)
    pallas_call x1, Pallas kernels, front_part(): pl.pallas_call(functools.partial(front_kernel, nn, nb), out_shape=(jax.Sh...  88.9 us
    pallas_call x1, Pallas kernels, last_part(): pl.pallas_call(last_kernel, out_shape=jax.ShapeDtypeStruct((3, ROWS, LX),...  20.8 us

profile of v1, /device:TPU:1, one launch (start us, length us, event | category | flops | bytes accessed | tf_op | source)
XLA Modules:
  0.0 111.4 jit_solution(2380519609981884620)
XLA Ops:
  0.0 1.5 %broadcast_in_dim.2.spacing = f32[384,128]{1,0:T(8,128)} broadcast(f32[384]{0:T(512)} %spacing.1), dimensions={0} | broadcast | bytes 198144 | tf_op jit(solution)/shard_map/broadcast_in_dim | solution.py:649
  1.5 88.9 %predict_solve.1 = (f32[3,6144,128]{2,1,0:T(8,128)}, f32[384,128]{1,0:T(8,128)}, f32[16,384,128]{2,1,0:T(8,128)}, f32[1024,128]{1,0:T(8,128)}) custom-call(f32[3,6144,128]{2,1,0:T(8,128)} %bitcast.2, f32[384]{0:T(512)} %spacing.1, f32[3]{0:T(128)} %eig.1, f32[384,384]{1,0:T(8,128)} %modes_hbm.1, bf16[256,256]{1,0:T(8,128)(2,1)} %constant.42.clone.xw_hbm, ...), custom_call_target="tpu_custom_call" | custom-call | tf_op jit(solution)/shard_map/predict_solve/pallas_call | solution.py:493
  90.4 20.8 %synthesis_correct.1 = f32[3,6144,128]{2,1,0:T(8,128)} custom-call(f32[16,384,128]{2,1,0:T(8,128)} %get-tuple-element.9.fh, f32[1024,128]{1,0:T(8,128)} %get-tuple-element.10.got, f32[384,128]{1,0:T(8,128)} %get-tuple-element.11.walls, f32[384,384]{1,0:T(8,128)} %from_modes.1, f32[384,128]{1,0:T(8,128)} %broadcast_in_dim.2.spacing, ...), custom_call_target="tpu_custom_call" | custom-call | tf_op jit(solution)/shard_map/synthesis_correct/pallas_call | solution.py:633

commit v2 on v1

--- a/solution.py
+++ b/solution.py
@@ -97,11 +97,12 @@
 
 def front_kernel(nn, nb, v_hbm, spacing, eig, modes_hbm, xw_hbm, edge_hl_hbm, edge_h_hbm, spec_h_hbm, spec_l_hbm,
                  back_h_hbm, back_l_hbm, mu_row, nu_lane, nu_row, mu_col, q_lane, turn_h, turn_l, unturn_h, unturn_l,
-                 cos_b, ex_row, star_hbm, walls, fh, got,
-                 v, star, rim, zsend, zrecv, xsend, xrecv, s2send, s2recv, x0send, x0recv,
-                 load_sem, store_sem, z_ss, z_rs, x_ss, x_rs, s2_ss, s2_rs, x0_ss, x0_rs, e_ss, e_rs,
+                 cos_b, ex_row, star_hbm, walls_hbm, pace_hbm, fh_hbm, got,
+                 v, star, rim, zsend, zrecv, xsend, xrecv, s2send, s2recv, x0send, x0recv, x1send, x1recv,
+                 load_sem, store_sem, z_ss, z_rs, x_ss, x_rs, s2_ss, s2_rs, x0_ss, x0_rs, x1_ss, x1_rs, e_ss, e_rs,
                  source, tiles, gz, gh, zl, zf, send, recv, back, s1, r1, s2, r2,
-                 to_modes, xw, edge_hl, edge_h, spec_h, spec_l, back_h, back_l, const_sem):
+                 to_modes, xw, edge_hl, edge_h, spec_h, spec_l, back_h, back_l, const_sem, edge, t_high, t_low,
+                 walls, pace, fh, out_sem):
     large = ((modes_hbm, to_modes), (xw_hbm, xw), (edge_hl_hbm, edge_hl), (edge_h_hbm, edge_h),
              (spec_h_hbm, spec_h), (spec_l_hbm, spec_l), (back_h_hbm, back_h), (back_l_hbm, back_l))
     me_n = lax.axis_index("narrow")
@@ -165,35 +166,47 @@
     lane = lax.broadcasted_iota(jnp.int32, (LZ, LX), 1)
     level = lax.broadcasted_iota(jnp.int32, (LZ, LX), 0)
 
-    def pack(ref, c, g):
+    def pack(ref, c, out):
         def step(yy, carry):
-            last, first = carry
-            plane = ref[c, pl.ds(pl.multiple_of(LZ + (g * LX + yy) * LZ, LZ), LZ), :]
-            turned = pltpu.roll(plane, lax.rem(yy + 1, LX), 1)
-            last = jnp.where(lane == yy, turned, last)
-            first = jnp.where(lane == lax.rem(yy + 1, LX), turned, first)
-            return last, first
-        last, first = lax.fori_loop(0, LX, step, (zero, zero), unroll=16)
-        return last, pltpu.roll(first, LX - 1, 1)
+            here, next_lane = lane == yy, lane == lax.rem(yy + 1, LX)
+            result = []
+            for g, (last, first) in enumerate(carry):
+                plane = ref[c, pl.ds(pl.multiple_of(LZ + (g * LX + yy) * LZ, LZ), LZ), :]
+                turned = pltpu.roll(plane, lax.rem(yy + 1, LX), 1)
+                result.append((jnp.where(here, turned, last), jnp.where(next_lane, turned, first)))
+            return tuple(result)
+        ends = lax.fori_loop(0, LX, step, ((zero, zero),) * GROUPS, unroll=16)
+        for g, (last, first) in enumerate(ends):
+            out[0, g] = last
+            out[1, g] = pltpu.roll(first, LX - 1, 1)
 
     share(spot_peers, me, 1, 0)
-    zcopies, xcopies = [], []
-    for c in (2, 0, 1):
-        loads[c].wait()
+    def outward_z(c, side):
+        return remote(zsend.at[side, c], zrecv.at[side, c], z_ss.at[side, c], z_rs.at[side, c], (up, down)[side])
+
+    def outward_x(c, side):
+        return remote(xsend.at[c, side], xrecv.at[side, c], x_ss.at[side, c], x_rs.at[side, c], (right, left)[side])
+
+    def component(i, _):
+        c = lax.rem(i + 2, 3)
+        pltpu.make_async_copy(v_hbm.at[c], v.at[c, pl.ds(LZ, ROWS)], load_sem.at[c]).wait()
+        pack(v, c, xsend.at[c])
+        for side in range(2):
+            outward_x(c, side).start()
+        return 0
+
+    def component_z(i, _):
+        c = lax.rem(i + 2, 3)
         zsend[0, c] = v[c, pl.ds(LZ + LZ - 1, NY, stride=LZ), :]
         zsend[1, c] = v[c, pl.ds(LZ, NY, stride=LZ), :]
-        for side, peer in ((0, up), (1, down)):
-            cp = remote(zsend.at[side, c], zrecv.at[side, c], z_ss.at[side, c], z_rs.at[side, c], peer)
-            cp.start()
-            zcopies.append(cp)
-        for g in range(GROUPS):
-            last, first = pack(v, c, g)
-            xsend[0, c, g] = last
-            xsend[1, c, g] = first
-        for side, peer in ((0, right), (1, left)):
-            cp = remote(xsend.at[side, c], xrecv.at[side, c], x_ss.at[side, c], x_rs.at[side, c], peer)
-            cp.start()
-            xcopies.append(cp)
+        for side in range(2):
+            outward_z(c, side).start()
+        return 0
+
+    lax.fori_loop(0, 3, component, 0)
+    lax.fori_loop(0, 3, component_z, 0)
+    zcopies = [outward_z(c, side) for c in range(3) for side in range(2)]
+    xcopies = [outward_x(c, side) for c in range(3) for side in range(2)]
 
     share_wait(spot_peers, 1, 0)
     share(layer_peers, me_n * nb + layer * ring, ring, 1)
@@ -245,88 +258,131 @@
 
     share_wait(layer_peers, ring, 1)
     share(narrow_peers, me_n * nb, nb, 2)
+    pack(star, 0, x0send)
+    x0copies = [remote(x0send.at[side], x0recv.at[side], x0_ss.at[side], x0_rs.at[side], peer)
+                for side, peer in ((0, right), (1, left))]
+    for cp in x0copies:
+        cp.start()
+    def pace_row(y, _):
+        pace[pl.ds(y, 1), :] = jnp.full((1, LX), spacing[y], jnp.float32)
+        return 0
+
+    lax.fori_loop(0, NY, pace_row, 0, unroll=8)
+    f32 = jnp.float32
+    nd = nn * nb
+    for cp in fetches:
+        cp.wait()
+    t_high[...], t_low[...] = split(to_modes[...])
+
+    def diverge_plane(y, odd):
+        g = y // LX
+        yy = lax.rem(y, LX)
+        base = pl.multiple_of(LZ + y * LZ, LZ)
+        s = 5.0 * spacing[y]
+        f = star[0, pl.ds(base, LZ), :]
+        east = jnp.where(lane == LX - 1, 0.0, pltpu.roll(f, LX - 1, 1))
+        west = jnp.where(lane == 0, 0.0, pltpu.roll(f, 1, 1))
+        north = star[2, pl.ds(base + 1, LZ), :]
+        south = star[2, pl.ds(base - 1, LZ), :]
+        rise = star[1, pl.ds(base + LZ, LZ), :] - star[1, pl.ds(base - LZ, LZ), :]
+        source[pl.ds(y, LZ, stride=NY), :] = 5.0 * ((east - west) + (north - south)) + s * rise
+
+    def diverge_pair(k, _):
+        diverge_plane(2 * k, 0)
+        diverge_plane(2 * k + 1, 1)
+        return 0
+
+    lax.fori_loop(0, NY // 2, diverge_pair, 0, unroll=8)
+
     for cp in zcopies:
         cp.wait_recv()
     part = 96
     for c in (2, 0, 1):
-        for k in range(NY // part):
-            hi = LZ + k * part * LZ + LZ - 1
+        def mend(k, _, c=c):
+            hi = LZ + LZ - 1 + k * part * LZ
             lo = LZ + k * part * LZ
-            rows = pl.ds(k * part, part)
+            rows = pl.ds(pl.multiple_of(k * part, 8), part)
             top = star[c, pl.ds(hi, part, stride=LZ), :] + zrecv[1, c, rows, :] * (
                 0.05 - 0.05 * v[2, pl.ds(hi, part, stride=LZ), :])
             low = star[c, pl.ds(lo, part, stride=LZ), :] + zrecv[0, c, rows, :] * (
                 0.05 + 0.05 * v[2, pl.ds(lo, part, stride=LZ), :])
+            if c == 2:
+                near_top = pl.ds(pl.multiple_of((LZ - 2) * NY + k * part, 8), part)
+                near_low = pl.ds(pl.multiple_of(NY + k * part, 8), part)
+                source[near_top, :] = source[near_top, :] + 5.0 * (top - star[c, pl.ds(hi, part, stride=LZ), :])
+                source[near_low, :] = source[near_low, :] - 5.0 * (low - star[c, pl.ds(lo, part, stride=LZ), :])
             star[c, pl.ds(hi, part, stride=LZ), :] = top
             star[c, pl.ds(lo, part, stride=LZ), :] = low
             if c == 2:
                 s2send[0, rows, :] = top
                 s2send[1, rows, :] = low
+            return 0
+
+        lax.fori_loop(0, NY // part, mend, 0)
         if c == 2:
             s2copies = [remote(s2send.at[side], s2recv.at[side], s2_ss.at[side], s2_rs.at[side], peer)
                         for side, peer in ((0, up), (1, down))]
             for cp in s2copies:
                 cp.start()
         if c == 0:
-            for g in range(GROUPS):
-                last, first = pack(star, 0, g)
-                x0send[0, g] = last
-                x0send[1, g] = first
-            x0copies = [remote(x0send.at[side], x0recv.at[side], x0_ss.at[side], x0_rs.at[side], peer)
+            pack(star, 0, x1send)
+            x1copies = [remote(x1send.at[side], x1recv.at[side], x1_ss.at[side], x1_rs.at[side], peer)
                         for side, peer in ((0, right), (1, left))]
-            for cp in x0copies:
+            for cp in x1copies:
                 cp.start()
     stores = [pltpu.make_async_copy(star.at[c, pl.ds(LZ, ROWS)], star_hbm.at[c], store_sem.at[c]) for c in range(3)]
     for cp in stores:
         cp.start()
     for cp in x0copies:
         cp.wait_recv()
+    middle = (level > 0) & (level < LZ - 1)
     for g in range(GROUPS):
-        rim[0, g, 0], rim[0, g, 1] = interleave(x0recv[1, g], x0recv[0, g])
-
-    def diverge_plane(y, odd):
-        g = y // LX
-        yy = lax.rem(y, LX)
-        base = pl.multiple_of(LZ + y * LZ, LZ)
-        s = 5.0 * spacing[y]
-        f = star[0, pl.ds(base, LZ), :]
-        ends = pltpu.roll(rim[0, g, odd], LX - 1 - yy, 1)
-        east = jnp.where(lane == LX - 1, ends, pltpu.roll(f, LX - 1, 1))
-        west = jnp.where(lane == 0, ends, pltpu.roll(f, 1, 1))
-        north = jnp.where(level == LZ - 1, 0.0, star[2, pl.ds(base + 1, LZ), :])
-        south = jnp.where(level == 0, 0.0, star[2, pl.ds(base - 1, LZ), :])
-        rise = star[1, pl.ds(base + LZ, LZ), :] - star[1, pl.ds(base - LZ, LZ), :]
-        source[pl.ds(y, LZ, stride=NY), :] = 5.0 * ((east - west) + (north - south)) + s * rise
-
-    def diverge_pair(k, _):
-        diverge_plane(2 * k, 0)
-        diverge_plane(2 * k + 1, 1)
-        return 0
-
-    lax.fori_loop(0, NY // 2, diverge_pair, 0, unroll=8)
-
-    f32 = jnp.float32
-    nd = nn * nb
-    for cp in fetches:
-        cp.wait()
-    t_high, t_low = split(to_modes[...])
-
-    def slabs(pair):
-        s_high, s_low = split(jnp.concatenate([source[pl.ds(z * NY, NY), :] for z in pair], axis=1))
-        modal = mm(t_high, s_high) + mm(t_low, s_high) + mm(t_high, s_low)
-        for k, z in enumerate(pair):
+        x0recv[0, g] = jnp.where(middle, -5.0 * x0recv[0, g], 0.0)
+        x0recv[1, g] = jnp.where(middle, 5.0 * x0recv[1, g], 0.0)
+    ridge = lax.broadcasted_iota(jnp.int32, (LX, LX), 0)
+
+    def whole(z):
+        columns = [jnp.transpose(jnp.where(ridge == 0, x0recv[0, g, pl.ds(z, 1), :],
+                                           jnp.where(ridge == LX - 1, x0recv[1, g, pl.ds(z, 1), :], 0.0)))
+                   for g in range(GROUPS)]
+        return source[pl.ds(pl.multiple_of(z * NY, LX), NY), :] + jnp.concatenate(columns, axis=0)
+
+    def finish_outer():
+        for cp in s2copies + x1copies:
+            cp.wait_recv()
+        square = lax.broadcasted_iota(jnp.int32, (LX, LX), 0)
+        lanes = lax.broadcasted_iota(jnp.int32, (LX, LX), 1)
+        for z, inner, sign, side in ((0, 1, 1.0, 0), (LZ - 1, LZ - 2, -1.0, 1)):
+            def rows_of(g, _, z=z, inner=inner, sign=sign, side=side):
+                first = LZ + z + g * (LX * LZ)
+                rows = pl.ds(pl.multiple_of(g * LX, LX), LX)
+                ends = jnp.transpose(jnp.where(square == 0, x1recv[0, g, z:z + 1, :], jnp.where(square == LX - 1, x1recv[1, g, z:z + 1, :], 0.0)))
+                f = star[0, pl.ds(first, LX, stride=LZ), :]
+                east = jnp.where(lanes == LX - 1, ends, pltpu.roll(f, LX - 1, 1))
+                west = jnp.where(lanes == 0, ends, pltpu.roll(f, 1, 1))
+                rise = star[1, pl.ds(first + LZ, LX, stride=LZ), :] - star[1, pl.ds(first - LZ, LX, stride=LZ), :]
+                across = sign * (star[2, pl.ds(first + inner - z, LX, stride=LZ), :] - s2recv[side, rows, :])
+                source[pl.ds(pl.multiple_of(z * NY + g * LX, LX), LX), :] = 5.0 * ((east - west) + across + pace[rows, :] * rise)
+                return 0
+
+            lax.fori_loop(0, GROUPS, rows_of, 0)
+
+    def slabs(i, _):
+        @pl.when(i == LZ // 2 - 2)
+        def _():
+            finish_outer()
+
+        p = lax.rem(i + 1, LZ // 2)
+        p = jnp.where(i == LZ // 2 - 2, LZ // 2 - 1, jnp.where(i == LZ // 2 - 1, 0, p))
+        s_high, s_low = split(jnp.concatenate([whole(2 * p), whole(2 * p + 1)], axis=1))
+        modal = mm(t_high[...], s_high) + mm(t_low[...], s_high) + mm(t_high[...], s_low)
+        for k in range(2):
             high, low = split(modal[:, k * LX:(k + 1) * LX])
             both = mm(jnp.concatenate([high, low], axis=1), xw[...])
-            gz[z] = both[:, :LX] + both[:, LX:]
-
-    for z in range(1, LZ - 1, 2):
-        slabs((z, z + 1))
-    for cp in s2copies:
-        cp.wait_recv()
-    low, top = pl.ds(0, NY), pl.ds((LZ - 1) * NY, NY)
-    source[low, :] = source[low, :] - 5.0 * s2recv[0]
-    source[top, :] = source[top, :] + 5.0 * s2recv[1]
-    slabs((0, LZ - 1))
+            gz[2 * p + k] = both[:, :LX] + both[:, LX:]
+        return 0
+
+    lax.fori_loop(0, LZ // 2, slabs, 0)
     share_wait(narrow_peers, nb, 2)
     each = NY // nd
     for k in range(each):
@@ -347,12 +403,16 @@
         zf[rows, :] = sums[0] - sums[1]
         return 0
 
-    lax.fori_loop(0, NY // 8, chunk, 0)
-    edge = jnp.zeros((NY, LX), f32)
-    for j in range(0, LZ, 2):
-        high, low = split(jnp.concatenate([gh[j], gh[j + 1]], axis=1))
-        both = mm(high, edge_hl[j // 2])
-        edge = edge + both[:, :LX] + both[:, LX:] + mm(low, edge_h[j // 2])
+    lax.fori_loop(0, NY // 8, chunk, 0, unroll=2)
+    edge[...] = jnp.zeros((NY, LX), f32)
+
+    def ends_of(j, _):
+        high, low = split(jnp.concatenate([gh[2 * j], gh[2 * j + 1]], axis=1))
+        both = mm(high, edge_hl[j])
+        edge[...] += both[:, :LX] + both[:, LX:] + mm(low, edge_h[j])
+        return 0
+
+    lax.fori_loop(0, LZ // 2, ends_of, 0)
     packed = edge[:nd]
     for r in range(R):
         rows = pl.ds(r * nd, nd)
@@ -379,6 +439,10 @@
                                             device_id=(me_n, me_b), device_id_type=MESH)
 
     out = ship(send, recv, s1, r1)
+    results = [pltpu.make_async_copy(m, h, out_sem.at[k])
+               for k, (m, h) in enumerate(((walls, walls_hbm), (pace, pace_hbm), (fh, fh_hbm)))]
+    for cp in results:
+        cp.start()
 
     own = [walls[pl.ds(r * nd + me, 1), :] for r in range(R)]
     lane = lax.broadcasted_iota(jnp.int32, (1, LX), 1)
@@ -459,9 +523,9 @@
     out.wait_send()
     home.wait_recv()
     home.wait_send()
-    for cp in zcopies + xcopies + s2copies + x0copies:
+    for cp in zcopies + xcopies + s2copies + x0copies + x1copies:
         cp.wait_send()
-    for cp in stores:
+    for cp in stores + results:
         cp.wait()
 
 
@@ -492,23 +556,25 @@
     dma = pltpu.SemaphoreType.DMA
     return pl.pallas_call(
         functools.partial(front_kernel, nn, nb),
-        out_shape=(jax.ShapeDtypeStruct((3, ROWS, LX), f32), jax.ShapeDtypeStruct((NY, LX), f32),
+        out_shape=(jax.ShapeDtypeStruct((3, ROWS, LX), f32), *[jax.ShapeDtypeStruct((NY, LX), f32)] * 2,
                    jax.ShapeDtypeStruct((LZ, NY, LX), f32), jax.ShapeDtypeStruct((nd * 8, LX), f32)),
         in_specs=[any_, smem, smem] + [any_] * (1 + len(big)) + [vmem] * len(small),
-        out_specs=(any_, vmem, vmem, vmem),
+        out_specs=(any_, any_, any_, any_, vmem),
         scratch_shapes=[
             pltpu.VMEM((3, ROWS + 2 * LZ, LX), f32), pltpu.VMEM((3, ROWS + 2 * LZ, LX), f32), pltpu.VMEM((3, GROUPS, 2, LZ, LX), f32),
             pltpu.VMEM((2, 3, NY, LX), f32), pltpu.VMEM((2, 3, NY, LX), f32),
-            pltpu.VMEM((2, 3, GROUPS, LZ, LX), f32), pltpu.VMEM((2, 3, GROUPS, LZ, LX), f32),
+            pltpu.VMEM((3, 2, GROUPS, LZ, LX), f32), pltpu.VMEM((2, 3, GROUPS, LZ, LX), f32),
             pltpu.VMEM((2, NY, LX), f32), pltpu.VMEM((2, NY, LX), f32),
-            pltpu.VMEM((2, GROUPS, LZ, LX), f32), pltpu.VMEM((2, GROUPS, LZ, LX), f32),
+            *[pltpu.VMEM((2, GROUPS, LZ, LX), f32)] * 4,
             dma((3,)), dma((3,)), dma((2, 3)), dma((2, 3)), dma((2, 3)), dma((2, 3)),
-            dma((2,)), dma((2,)), dma((2,)), dma((2,)), dma((3,)), dma((3,)),
+            *[dma((2,))] * 6, dma((3,)), dma((3,)),
             pltpu.VMEM((LZ * NY, LX), f32), pltpu.VMEM((nd * 8, LX), f32),
             pltpu.VMEM((LZ, NY, LX), f32), pltpu.VMEM((LZ, NY, LX), f32), pltpu.VMEM((NY, LX), f32), pltpu.VMEM((NY, LX), f32),
             pltpu.VMEM((nd * 8, LX), f32), pltpu.VMEM((nd * 8, LX), f32), pltpu.VMEM((nd * 8, LX), f32),
             dma, dma, dma, dma,
             pltpu.VMEM((NY, NY), f32), *[pltpu.VMEM(a.shape, jnp.bfloat16) for a in big], dma((1 + len(big),)),
+            pltpu.VMEM((NY, LX), f32), pltpu.VMEM((NY, NY), jnp.bfloat16), pltpu.VMEM((NY, NY), jnp.bfloat16),
+            pltpu.VMEM((NY, LX), f32), pltpu.VMEM((NY, LX), f32), pltpu.VMEM((LZ, NY, LX), f32), dma((3,)),
         ],
         compiler_params=pltpu.CompilerParams(collective_id=0, has_side_effects=True, vmem_limit_bytes=60 * 1024 * 1024),
         name="predict_solve",
@@ -645,8 +711,7 @@
 
 
 def shards(velocity, inv_spacing, eigen_wall, to_modes, from_modes):
-    star, walls, fh, got = front_part(velocity, inv_spacing, eigen_wall, to_modes)
-    spacing = jnp.broadcast_to(inv_spacing[:, None], (NY, LX))
+    star, walls, spacing, fh, got = front_part(velocity, inv_spacing, eigen_wall, to_modes)
     return last_part(fh, got, walls, from_modes, spacing, star).reshape(3, NY, LZ, LX)
 
 

time: 112 us -> 104 us (0.929)
  Pallas kernels: 110 us -> 104 us
  local copies, waits for them, and re-layouts: 1.48 us -> 0 us
    pallas_call x1, Pallas kernels: 88.9 us -> 83.4 us  [front_part(): pl.pallas_call(functools.partial(front_kernel, nn, nb), out_shape=(jax.Sh...]
    broadcast_in_dim x1 -> x0, local copies, waits for them, and re-layouts: 1.48 us -> none  [shards(): spacing = jnp.broadcast_to(inv_spacing[:, None], (NY, LX))]
where the time goes in v2:
time: 104 us
  Pallas kernels  104 us (100%)
    pallas_call x1, Pallas kernels, front_part(): pl.pallas_call(functools.partial(front_kernel, nn, nb), out_shape=(jax.Sh...  83.4 us
    pallas_call x1, Pallas kernels, last_part(): pl.pallas_call(last_kernel, out_shape=jax.ShapeDtypeStruct((3, ROWS, LX),...  20.7 us

profile of v2, /device:TPU:1, one launch (start us, length us, event | category | flops | bytes accessed | tf_op | source)
XLA Modules:
  0.0 104.1 jit_solution(12959388132843872591)
XLA Ops:
  0.0 83.4 %predict_solve.1 = (f32[3,6144,128]{2,1,0:T(8,128)}, f32[384,128]{1,0:T(8,128)}, f32[384,128]{1,0:T(8,128)}, f32[16,384,128]{2,1,0:T(8,128)}, f32[1024,128]{1,0:T(8,128)}) custom-call(f32[3,6144,128]{2,1,0:T(8,128)} %bitcast.2, f32[384]{0:T(512)} %spacing.1, f32[3]{0:T(128)} %eig.1, f32[384,384]{1,0:T(8,128)} %modes_hbm.1, ...), custom_call_target="tpu_custom_call" | custom-call | tf_op jit(solution)/shard_map/predict_solve/pallas_call | solution.py:557
  83.4 20.7 %synthesis_correct.1 = f32[3,6144,128]{2,1,0:T(8,128)} custom-call(f32[16,384,128]{2,1,0:T(8,128)} %get-tuple-element.10.fh, f32[1024,128]{1,0:T(8,128)} %get-tuple-element.11.got, f32[384,128]{1,0:T(8,128)} %get-tuple-element.12.walls, f32[384,384]{1,0:T(8,128)} %from_modes.1, f32[384,128]{1,0:T(8,128)} %get-tuple-element.13.spacing, ...), custom_call_target="tpu_custom_call" | custom-call | tf_op jit(solution)/shard_map/synthesis_correct/pallas_call | solution.py:699

commit v3 on v2

--- a/solution.py
+++ b/solution.py
@@ -254,7 +254,7 @@
         predict_plane(2 * k + 1, 1)
         return 0
 
-    lax.fori_loop(0, NY // 2, predict_pair, 0, unroll=8)
+    lax.fori_loop(0, NY // 2, predict_pair, 0, unroll=12)
 
     share_wait(layer_peers, ring, 1)
     share(narrow_peers, me_n * nb, nb, 2)
@@ -292,7 +292,7 @@
         diverge_plane(2 * k + 1, 1)
         return 0
 
-    lax.fori_loop(0, NY // 2, diverge_pair, 0, unroll=8)
+    lax.fori_loop(0, NY // 2, diverge_pair, 0, unroll=16)
 
     for cp in zcopies:
         cp.wait_recv()

time: 104 us -> 104 us (level)
  no operation moved by 1% of the time
where the time goes in v3:
time: 104 us; the launch traced here: 103 us
  Pallas kernels  103 us (99%)
    pallas_call x1, Pallas kernels, front_part(): pl.pallas_call(functools.partial(front_kernel, nn, nb), out_shape=(jax.Sh...  82.7 us
    pallas_call x1, Pallas kernels, last_part(): pl.pallas_call(last_kernel, out_shape=jax.ShapeDtypeStruct((3, ROWS, LX),...  20.7 us

profile of v3, /device:TPU:1, one launch (start us, length us, event | category | flops | bytes accessed | tf_op | source)
XLA Modules:
  0.0 103.4 jit_solution(13740930791940761615)
XLA Ops:
  0.0 82.7 %predict_solve.1 = (f32[3,6144,128]{2,1,0:T(8,128)}, f32[384,128]{1,0:T(8,128)}, f32[384,128]{1,0:T(8,128)}, f32[16,384,128]{2,1,0:T(8,128)}, f32[1024,128]{1,0:T(8,128)}) custom-call(f32[3,6144,128]{2,1,0:T(8,128)} %bitcast.2, f32[384]{0:T(512)} %spacing.1, f32[3]{0:T(128)} %eig.1, f32[384,384]{1,0:T(8,128)} %modes_hbm.1, ...), custom_call_target="tpu_custom_call" | custom-call | tf_op jit(solution)/shard_map/predict_solve/pallas_call | solution.py:557
  82.7 20.7 %synthesis_correct.1 = f32[3,6144,128]{2,1,0:T(8,128)} custom-call(f32[16,384,128]{2,1,0:T(8,128)} %get-tuple-element.10.fh, f32[1024,128]{1,0:T(8,128)} %get-tuple-element.11.got, f32[384,128]{1,0:T(8,128)} %get-tuple-element.12.walls, f32[384,384]{1,0:T(8,128)} %from_modes.1, f32[384,128]{1,0:T(8,128)} %get-tuple-element.13.spacing, ...), custom_call_target="tpu_custom_call" | custom-call | tf_op jit(solution)/shard_map/synthesis_correct/pallas_call | solution.py:699
